TPU v7x, 128 devices: a whole 4x4x4 slice. The times are simulated.
128 devices in a mesh: ctx: 64 (over x, y, z_hi, core), wa: 2 (over z_lo).
Axes of the slice: x: 4, y: 4, z: 4 (z_hi: 2, z_lo: 2; z = z_hi * 2 + z_lo), core: 2. Of those that a mesh axis runs over, the one named last changes fastest.
Arguments:
- tokens: bfloat16 [8192, 768], P('ctx'), may hold values from -6 to 6
- doc_start: int32 [8192], P('ctx'), may hold values from 0 to 8191, as said below
- exit_layer: int32 [8192], P('ctx'), may hold values from 1 to 12, as said below
- cotangent: bfloat16 [8192, 768], P('ctx'), may hold values from -6 to 6
- ln1_gain: float32 [768], replicated, may hold values from 0.25 to 1.75
- ln1_shift: float32 [768], replicated, may hold values from -1.5 to 1.5
- q_weight: bfloat16 [768, 768], P(None, 'wa'), may hold values from -0.3125 to 0.3125
- q_bias: float32 [768], P('wa'), may hold values from -1.5 to 1.5
- k_weight: bfloat16 [768, 768], P(None, 'wa'), may hold values from -0.3125 to 0.3125
- v_weight: bfloat16 [768, 768], P(None, 'wa'), may hold values from -0.21875 to 0.21875
- v_bias: float32 [768], P('wa'), may hold values from -1.5 to 1.5
- o_weight: bfloat16 [768, 768], P('wa'), may hold values from -1.75 to 1.75
- o_bias: float32 [768], replicated, may hold values from -1.5 to 1.5
- ln2_gain: float32 [768], replicated, may hold values from 0.25 to 1.75
- ln2_shift: float32 [768], replicated, may hold values from -1.5 to 1.5
- up_weight: bfloat16 [768, 3072], P(None, 'wa'), may hold values from -0.21875 to 0.21875
- up_bias: float32 [3072], P('wa'), may hold values from -1.5 to 1.5
- down_weight: bfloat16 [3072, 768], P('wa'), may hold values from -0.15625 to 0.15625
- down_bias: float32 [768], replicated, may hold values from -1.5 to 1.5
Outputs:
- output: bfloat16 [8192, 768], P('ctx')
- input_grad: float32 [8192, 768], P('ctx')
- ln1_gain_grad: float32 [768], replicated
- ln1_shift_grad: float32 [768], replicated
- q_weight_grad: float32 [768, 768], P('ctx', 'wa')
- q_bias_grad: float32 [768], P('wa')
- k_weight_grad: float32 [768, 768], P('ctx', 'wa')
- v_weight_grad: float32 [768, 768], P('ctx', 'wa')
- v_bias_grad: float32 [768], P('wa')
- o_weight_grad_t: float32 [768, 768], P('ctx', 'wa')
- o_bias_grad: float32 [768], replicated
- ln2_gain_grad: float32 [768], replicated
- ln2_shift_grad: float32 [768], replicated
- up_weight_grad: float32 [768, 3072], P('ctx', 'wa')
- up_bias_grad: float32 [3072], P('wa')
- down_weight_grad_t: float32 [768, 3072], P('ctx', 'wa')
- down_bias_grad: float32 [768], replicated
Inputs may be any that keep to these rules, and one draw needn't show every extreme that they name: doc_start(k) is the stream position at which the document holding place(k) begins; documents are contiguous runs of the stream of 1 to 4096 positions; one of exactly 4096 positions begins among the first 64 positions of the stream, and the stream's last position is a document of its own. `exit_layer`: within a document, exit layers never increase along the stream, and a document's first position has exit layer 12, so the active positions of each document form a non-empty prefix of it; every position of the document of 4096 positions that begins among the first 64 is active.
All inputs are finite; a program needn't handle non-finite values.
Results may differ from a plain program's by a relative error of at most 0.014.
The roundings to bfloat16 on the way count: a program that leaves them out, or rounds other values in their place, can miss the bound.
Values may be sent and summed in bfloat16 or wider, within the bound.
No kernel may reach another device: no remote copies, remote signals or barrier semaphores. Data moves between devices by JAX's collectives and lax.ppermute only.
A program may use at most 192 MiB of HBM per device.

v0:
```python
import math

import jax
import jax.numpy as jnp
from jax import lax
from jax.sharding import PartitionSpec as P

HEAD_DIM = 64
LAYER = 6


epsilon = 1e-05
trans_right = (((1,), (1,)), ((), ()))
trans_left = (((0,), (0,)), ((), ()))
sub_rows = 2048
cubic_coef = 0.044715


def gelu_pair(values):
    outer = math.sqrt(2.0 / math.pi)
    inner = outer * (values + cubic_coef * values * values * values)
    tangent = jnp.tanh(inner)
    result = 0.5 * values * (1.0 + tangent)
    gelu_slope = 0.5 * (1.0 + tangent) + 0.5 * values * (1.0 - tangent * tangent) * outer * (
        1.0 + 3.0 * cubic_coef * values * values
    )
    return (result, gelu_slope)


def stream_place(row_ids, per_device, stream_len):
    half_rows = per_device // 2
    device = row_ids // per_device
    within = row_ids % per_device
    return jnp.where(
        within < half_rows,
        device * half_rows + within,
        stream_len - (device + 1) * half_rows + within - half_rows,
    )


def norm_forward(values, gain_vec, shift_vec):
    average = jnp.mean(values, axis=-1, keepdims=True)
    centred = values - average
    inverse_std = lax.rsqrt(jnp.mean(centred * centred, axis=-1, keepdims=True) + epsilon)
    normed = centred * inverse_std
    return (normed * gain_vec + shift_vec, normed, inverse_std)


def norm_backward(grad_out, normed, inverse_std, gain_vec):
    scaled = grad_out * gain_vec
    return inverse_std * (
        scaled
        - jnp.mean(scaled, axis=-1, keepdims=True)
        - normed * jnp.mean(scaled * normed, axis=-1, keepdims=True)
    )


def by_blocks(step_fn, running, row_total):

    def one_step(index, state):
        return step_fn(state, index * sub_rows, sub_rows)

    return lax.fori_loop(0, row_total // sub_rows, one_step, running)


def attend_block(query_rows, key_rows, visible, scaling):
    scores = (
        jnp.einsum("qhd,khd->hqk", query_rows, key_rows, preferred_element_type=jnp.float32)
        * scaling
    )
    return jnp.where(visible[None], jnp.exp(scores), 0.0)


def block_grads(query_rows, dhead_rows, denoms, row_dot, key_rows, value_rows, visible, scaling):
    expweights = attend_block(query_rows, key_rows, visible, scaling)
    reciprocal = 1.0 / denoms
    dprob = jnp.einsum("qhd,khd->hqk", dhead_rows, value_rows, preferred_element_type=jnp.float32)
    dscore = (expweights * (dprob - row_dot.T[:, :, None]) * reciprocal.T[:, :, None]).astype(
        jnp.bfloat16
    )
    query_grad = (
        jnp.einsum("hqk,khd->qhd", dscore, key_rows, preferred_element_type=jnp.float32) * scaling
    )
    key_grad = (
        jnp.einsum("hqk,qhd->khd", dscore, query_rows, preferred_element_type=jnp.float32) * scaling
    )
    dnumer = dhead_rows.astype(jnp.float32) * reciprocal[:, :, None]
    upper_part = dnumer.astype(jnp.bfloat16)
    lower_part = (dnumer - upper_part.astype(jnp.float32)).astype(jnp.bfloat16)
    rounded = expweights.astype(jnp.bfloat16)
    value_grad = jnp.einsum(
        "hqk,qhd->khd", rounded, upper_part, preferred_element_type=jnp.float32
    ) + jnp.einsum("hqk,qhd->khd", rounded, lower_part, preferred_element_type=jnp.float32)
    return (query_grad, key_grad, value_grad)


def on_device(
    tokens,
    doc_start,
    exit_layer,
    cotangent,
    ln1_gain,
    ln1_shift,
    q_weight,
    q_bias,
    k_weight,
    v_weight,
    v_bias,
    o_weight,
    o_bias,
    ln2_gain,
    ln2_shift,
    up_weight,
    up_bias,
    down_weight,
    down_bias,
):
    per_device, model_width = tokens.shape
    cycle_size = lax.axis_size("ctx")
    stream_len = per_device * cycle_size
    local_width = q_weight.shape[1]
    local_heads = local_width // HEAD_DIM
    local_hidden = up_weight.shape[1]
    scaling = 1.0 / math.sqrt(HEAD_DIM)
    cycle_index = lax.axis_index("ctx")
    own_rows = cycle_index * per_device + jnp.arange(per_device, dtype=jnp.int32)
    query_place = stream_place(own_rows, per_device, stream_len)
    active = exit_layer > LAYER
    stream_in = tokens.astype(jnp.float32)
    normed_one, unit_one, inv_one = norm_forward(stream_in, ln1_gain, ln1_shift)
    lowered_one = normed_one.astype(jnp.bfloat16)
    queries = (jnp.dot(lowered_one, q_weight, preferred_element_type=jnp.float32) + q_bias).astype(
        jnp.bfloat16
    )
    keyset = jnp.dot(lowered_one, k_weight, preferred_element_type=jnp.float32).astype(jnp.bfloat16)
    valueset = (jnp.dot(lowered_one, v_weight, preferred_element_type=jnp.float32) + v_bias).astype(
        jnp.bfloat16
    )
    query_heads = queries.reshape(per_device, local_heads, HEAD_DIM)
    key_value = jnp.concatenate([keyset, valueset], axis=1)

    def split_pairs(rows_kv):
        row_total = rows_kv.shape[0]
        return (
            rows_kv[:, :local_width].reshape(row_total, local_heads, HEAD_DIM),
            rows_kv[:, local_width:].reshape(row_total, local_heads, HEAD_DIM),
        )

    def key_visible(begin_row, row_total):
        key_place = stream_place(
            begin_row + jnp.arange(row_total, dtype=jnp.int32), per_device, stream_len
        )
        return (key_place[None, :] >= doc_start[:, None]) & (
            key_place[None, :] <= query_place[:, None]
        )

    start_state = (
        jnp.zeros((per_device, local_heads, HEAD_DIM), jnp.float32),
        jnp.zeros((per_device, local_heads), jnp.float32),
    )
    shard_rows = lax.all_gather(key_value, "ctx", axis=0, tiled=True)

    def step_fn(state, offset, size_rows):
        block_kv = lax.dynamic_slice_in_dim(shard_rows, offset, size_rows, 0)
        key_rows, value_rows = split_pairs(block_kv)
        visible = key_visible(offset, size_rows)

        def accumulate(inner):
            numer_acc, denom_acc = inner
            expweights = attend_block(query_heads, key_rows, visible, scaling)
            numer_acc = numer_acc + jnp.einsum(
                "hqk,khd->qhd",
                expweights.astype(jnp.bfloat16),
                value_rows,
                preferred_element_type=jnp.float32,
            )
            return (numer_acc, denom_acc + jnp.sum(expweights, axis=-1).T)

        return accumulate(state)

    numerator, denominators = by_blocks(step_fn, start_state, shard_rows.shape[0])
    attn_full = numerator / denominators[:, :, None]
    attn_low = attn_full.reshape(per_device, local_width).astype(jnp.bfloat16)
    attn_out = (
        lax.psum(jnp.dot(attn_low, o_weight, preferred_element_type=jnp.float32), "wa") + o_bias
    )
    middle = stream_in + attn_out
    normed_two, unit_two, inv_two = norm_forward(middle, ln2_gain, ln2_shift)
    lowered_two = normed_two.astype(jnp.bfloat16)
    pre_act = jnp.dot(lowered_two, up_weight, preferred_element_type=jnp.float32) + up_bias
    hidden_full, gelu_slope = gelu_pair(pre_act)
    hidden = hidden_full.astype(jnp.bfloat16)
    ffn_out = (
        lax.psum(
            jnp.dot(hidden, down_weight, preferred_element_type=jnp.float32).astype(jnp.bfloat16),
            "wa",
        ).astype(jnp.float32)
        + down_bias
    )
    output = jnp.where(active[:, None], middle + ffn_out, stream_in).astype(jnp.bfloat16)
    cot_stream = cotangent.astype(jnp.float32)
    branch_grad = jnp.where(active[:, None], cot_stream, 0.0)
    branch_low = branch_grad.astype(jnp.bfloat16)
    dhidden = lax.dot_general(
        branch_low, down_weight, trans_right, preferred_element_type=jnp.float32
    )
    dpre_low = (dhidden * gelu_slope).astype(jnp.bfloat16)
    dnormed_two = lax.psum(
        lax.dot_general(dpre_low, up_weight, trans_right, preferred_element_type=jnp.float32), "wa"
    )
    dmiddle = branch_grad + norm_backward(dnormed_two, unit_two, inv_two, ln2_gain)
    dattn_low = dmiddle.astype(jnp.bfloat16)
    dheads_low = lax.dot_general(
        dattn_low, o_weight, trans_right, preferred_element_type=jnp.float32
    ).astype(jnp.bfloat16)
    dhead_heads = dheads_low.reshape(per_device, local_heads, HEAD_DIM)
    row_dot = jnp.sum(dhead_heads.astype(jnp.float32) * attn_full, axis=-1)
    back_state = (
        jnp.zeros((per_device, local_heads, HEAD_DIM), jnp.float32),
        jnp.zeros((stream_len, 2 * local_width), jnp.float32),
    )
    key_shard_rows = lax.all_gather(key_value, "ctx", axis=0, tiled=True)

    def step_fn(state, offset, size_rows):
        block_kv = lax.dynamic_slice_in_dim(key_shard_rows, offset, size_rows, 0)
        key_rows, value_rows = split_pairs(block_kv)
        target = offset
        visible = key_visible(target, size_rows)

        def accumulate(inner):
            query_acc, pair_all = inner
            query_grad, key_grad, value_grad = block_grads(
                query_heads,
                dhead_heads,
                denominators,
                row_dot,
                key_rows,
                value_rows,
                visible,
                scaling,
            )
            addend = jnp.concatenate(
                [
                    key_grad.reshape(size_rows, local_width),
                    value_grad.reshape(size_rows, local_width),
                ],
                axis=1,
            )
            previous = lax.dynamic_slice_in_dim(pair_all, target, size_rows, 0)
            return (
                query_acc + query_grad,
                lax.dynamic_update_slice_in_dim(pair_all, previous + addend, target, 0),
            )

        return accumulate(state)

    query_acc, pair_all = by_blocks(step_fn, back_state, key_shard_rows.shape[0])
    pair_sum = lax.psum_scatter(pair_all, "ctx", scatter_dimension=0, tiled=True)
    query_sum = query_acc.reshape(per_device, local_width)
    query_low = query_sum.astype(jnp.bfloat16)
    key_low = pair_sum[:, :local_width].astype(jnp.bfloat16)
    value_low = pair_sum[:, local_width:].astype(jnp.bfloat16)
    dnormed_part = (
        lax.dot_general(query_low, q_weight, trans_right, preferred_element_type=jnp.float32)
        + lax.dot_general(key_low, k_weight, trans_right, preferred_element_type=jnp.float32)
        + lax.dot_general(value_low, v_weight, trans_right, preferred_element_type=jnp.float32)
    )
    dnormed_one = lax.psum(dnormed_part.astype(jnp.bfloat16), "wa").astype(jnp.float32)
    input_grad = (
        dmiddle
        + norm_backward(dnormed_one, unit_one, inv_one, ln1_gain)
        + jnp.where(active[:, None], 0.0, cot_stream)
    )
    small_terms = (
        jnp.sum(query_low.astype(jnp.float32), axis=0),
        jnp.sum(value_low.astype(jnp.float32), axis=0),
        jnp.sum(dpre_low.astype(jnp.float32), axis=0),
        jnp.sum(dattn_low.astype(jnp.float32), axis=0),
        jnp.sum(branch_grad, axis=0),
        jnp.sum(dnormed_one * unit_one, axis=0),
        jnp.sum(dnormed_one, axis=0),
        jnp.sum(dnormed_two * unit_two, axis=0),
        jnp.sum(dnormed_two, axis=0),
    )
    (
        q_bias_grad,
        v_bias_grad,
        up_bias_grad,
        o_bias_grad,
        down_bias_grad,
        ln1_gain_grad,
        ln1_shift_grad,
        ln2_gain_grad,
        ln2_shift_grad,
    ) = lax.psum(
        (
            small_terms[0],
            small_terms[1],
            small_terms[2],
            small_terms[3],
            small_terms[4],
            small_terms[5],
            small_terms[6],
            small_terms[7],
            small_terms[8],
        ),
        "ctx",
    )
    weight_sums = lax.psum_scatter(
        jnp.concatenate(
            [
                lax.dot_general(
                    lowered_one, query_low, trans_left, preferred_element_type=jnp.float32
                ),
                lax.dot_general(
                    lowered_one, key_low, trans_left, preferred_element_type=jnp.float32
                ),
                lax.dot_general(
                    lowered_one, value_low, trans_left, preferred_element_type=jnp.float32
                ),
                lax.dot_general(
                    dattn_low, attn_low, trans_left, preferred_element_type=jnp.float32
                ),
                lax.dot_general(
                    lowered_two, dpre_low, trans_left, preferred_element_type=jnp.float32
                ),
                lax.dot_general(branch_low, hidden, trans_left, preferred_element_type=jnp.float32),
            ],
            axis=1,
        ),
        "ctx",
        scatter_dimension=0,
        tiled=True,
    )
    q_weight_grad = weight_sums[:, :local_width]
    k_weight_grad = weight_sums[:, local_width : 2 * local_width]
    v_weight_grad = weight_sums[:, 2 * local_width : 3 * local_width]
    o_weight_grad_t = weight_sums[:, 3 * local_width : 4 * local_width]
    up_weight_grad = weight_sums[:, 4 * local_width : 4 * local_width + local_hidden]
    down_weight_grad_t = weight_sums[:, 4 * local_width + local_hidden :]
    return (
        output,
        input_grad,
        ln1_gain_grad,
        ln1_shift_grad,
        q_weight_grad,
        q_bias_grad,
        k_weight_grad,
        v_weight_grad,
        v_bias_grad,
        o_weight_grad_t,
        o_bias_grad,
        ln2_gain_grad,
        ln2_shift_grad,
        up_weight_grad,
        up_bias_grad,
        down_weight_grad_t,
        down_bias_grad,
    )


def solution(mesh):
    return jax.shard_map(
        on_device,
        mesh=mesh,
        in_specs=(
            P("ctx", None),
            P("ctx"),
            P("ctx"),
            P("ctx", None),
            P(),
            P(),
            P(None, "wa"),
            P("wa"),
            P(None, "wa"),
            P(None, "wa"),
            P("wa"),
            P("wa", None),
            P(),
            P(),
            P(),
            P(None, "wa"),
            P("wa"),
            P("wa", None),
            P(),
        ),
        out_specs=(
            P("ctx", None),
            P("ctx", None),
            P(),
            P(),
            P("ctx", "wa"),
            P("wa"),
            P("ctx", "wa"),
            P("ctx", "wa"),
            P("wa"),
            P("ctx", "wa"),
            P(),
            P(),
            P(),
            P("ctx", "wa"),
            P("wa"),
            P("ctx", "wa"),
            P(),
        ),
        check_vma=False,
    )
```

profile of v0, /device:TPU:1, one launch (start us, length us, event | category | flops | bytes accessed | tf_op | source)
XLA Modules:
  0.0 1356.7 jit_solution(6368356368555515332)
XLA Ops:
  15.0 96.1 %all-gather.2.cloned.1.call-done = bf16[8192,768]{1,0:T(8,128)(2,1)} async-done(((bf16[128,768]{1,0:T(8,128)(2,1)}), bf16[8192,768]{1,0:T(8,128)(2,1)}) %all-gather.2.cloned.1.call-update) | async-done | bytes 12582928 | tf_op jit(solution)/shard_map/all_gather | solution.py:161
  111.1 16.0 %copy.70 = bf16[8192,768]{0,1:T(8,128)(2,1)} copy(bf16[8192,768]{1,0:T(8,128)(2,1)} %all-gather.2.cloned.1.call-done) | data formatting | bytes 25165824
  127.2 52.2 %while.36 = (s32[]{:T(128)}, f32[128,6,64]{0,2,1:T(8,128)S(1)}, f32[128,6]{0,1:T(8,128)S(1)}, bf16[8192,768]{0,1:T(8,128)(2,1)}, s32[128]{0:T(128)S(1)}, /*index...) while((s32[]{:T(128)}, f32[128,6,64]{0,2,1:T(8,128)S(1)}, ...), condition=%wide.region_4.5_spmd.clone, body=%wide.region_2.4_spmd.clone.sunk | while | flops 413038976 | bytes 23328464 | solution.py:63
  127.2 3.5 constant_dynamic-slice_fusion.4
  131.1 4.5 fusion.158
  135.7 4.6 fusion.159
  140.3 3.4 constant_dynamic-slice_fusion.4
  144.2 4.5 fusion.158
  148.7 4.7 fusion.159
  153.4 3.4 constant_dynamic-slice_fusion.4
  157.2 4.5 fusion.158
  161.7 4.7 fusion.159
  166.4 3.4 constant_dynamic-slice_fusion.4
  170.2 4.5 fusion.158
  174.7 4.7 fusion.159
  179.5 2.2 fusion.99
  181.8 29.6 %all-reduce.8.cloned.1.call-done = f32[128,768]{1,0:T(8,128)} async-done(((f32[128,768]{1,0:T(8,128)}), f32[128,768]{1,0:T(8,128)}) %all-reduce.8.cloned.1.call-update) | async-done | bytes 393232 | tf_op jit(solution)/shard_map/psum | solution.py:185
  212.9 2.2 convolution_add_fusion.1
  219.7 33.3 %all-reduce.10.cloned.1.call-done = f32[128,768]{1,0:T(8,128)} async-done(((f32[128,768]{1,0:T(8,128)}), f32[128,768]{1,0:T(8,128)}) %all-reduce.10.cloned.1.call-update) | async-done | bytes 393232 | tf_op jit(solution)/shard_map/psum | solution.py:208
  258.8 11.4 broadcast_in_dim.155
  270.2 110.9 %while.37 = (s32[]{:T(128)}, f32[128,6,64]{0,2,1:T(8,128)}, f32[8192,768]{0,1:T(8,128)}, bf16[8192,768]{0,1:T(8,128)(2,1)}, s32[128]{0:T(128)S(1)}, /*index=5*/b...) while((s32[]{:T(128)}, f32[128,6,64]{0,2,1:T(8,128)}, ...), condition=%wide.region_14.15_spmd.clone, body=%wide.region_13.14_spmd.clone.sunk | while | flops 1232992640 | bytes 141958000 | solution.py:63
  270.2 2.2 fusion.171
  275.1 4.3 fusion.173
  279.4 3.9 fusion.174
  283.3 4.3 fusion.175
  290.7 7.3 fusion.176
  298.0 2.2 fusion.171
  302.9 4.3 fusion.173
  307.1 3.9 fusion.174
  311.0 4.3 fusion.175
  318.4 7.2 fusion.176
  330.6 4.3 fusion.173
  334.9 3.9 fusion.174
  338.7 4.3 fusion.175
  346.1 7.2 fusion.176
  358.3 4.3 fusion.173
  362.5 3.9 fusion.174
  366.4 4.3 fusion.175
  373.8 7.3 fusion.176
  381.4 2.4 convolution_convert_fusion
  387.7 228.8 %reduce-scatter.2.cloned.1.call-done = f32[128,768]{0,1:T(8,128)} async-done(((f32[8192,768]{0,1:T(8,128)}), f32[128,768]{0,1:T(8,128)}) %reduce-scatter.2.cloned.1.call-update) | async-done | bytes 393232 | tf_op jit(solution)/shard_map/reduce_scatter | solution.py:258
  624.2 2.5 convolution_dynamic-update-slice_fusion.2
  626.8 4.0 convolution_dynamic-update-slice_fusion.1
  630.8 4.2 convolution_dynamic-update-slice_fusion
  637.1 21.2 %all-reduce.14.cloned.1.call-done = (bf16[128,768]{1,0:T(8,128)(2,1)}, bf16[128,768]{1,0:T(8,128)(2,1)}) async-done(((bf16[128,768]{1,0:T(8,128)(2,1)}, bf16[128,768]{1,0:T(8,128)(2,1)}), (bf16[128,768]{1,0:T(8,128)(2,1)}, bf16[128,768]{1,0:T(8,128)(2,1)})) %all-reduce.14.cloned.1.call-update) | async-done | bytes 393232 | tf_op jit(solution)/shard_map/psum | solution.py:194
  659.4 324.3 %all-reduce.1 = (f32[768]{0:T(1024)}, f32[768]{0:T(1024)}, f32[384]{0:T(512)}, f32[384]{0:T(512)}, f32[768]{0:T(1024)}, /*index=5*/f32[768]{0:T(1024)}, f32[768]{0:T(1024)}, f32[1536]{0:T(1024)}, f32[768]{0:T(1024)}) all-reduce(f32[768]{0:T(1024)S(1)} %get-tuple-element.566, ...), channel_id=1, replica_groups=mesh['ctx'=64,'wa'=2] {'ctx'}, use_global_device_ids=true, to_apply=%region_20.21 | all-reduce | flops 6912 | bytes 55296 | tf_op jit(solution)/shard_map/psum | solution.py:295
  983.8 2.2 fusion.71
  986.0 360.5 %all-reduce.12.cloned.1.call-done = f32[768,4608]{1,0:T(8,128)} async-done(((f32[768,4608]{1,0:T(8,128)}), f32[768,4608]{1,0:T(8,128)}) %all-reduce.12.cloned.1.call-update) | async-done | bytes 14155792
  (196 shorter events, 66.5 us)
Async XLA Ops:
  7.2 208.8 %copy-start = (bf16[1536,768]{1,0:T(8,128)(2,1)S(1)}, bf16[1536,768]{1,0:T(8,128)(2,1)}, u32[]{:S(2)}) copy-start(bf16[1536,768]{1,0:T(8,128)(2,1)} %param.40) | copy-start | bytes 7077892
  7.2 103.9 %all-gather.2.cloned.1.call-start = ((), (), s32[]{:S(2)}) async-start(), calls=%async_computation.1 | async-start | bytes 12779520 | tf_op jit(solution)/shard_map/all_gather | solution.py:161
  8.4 118.7 %copy-start.19 = (f32[128]{0:T(128)}, f32[128]{0:T(128)S(1)}, u32[]{:S(2)}) copy-start(f32[128]{0:T(128)S(1)} %broadcast_multiply_fusion.5) | copy-start | bytes 1540
  9.6 117.5 %copy-start.22 = (f32[128]{0:T(128)}, f32[128]{0:T(128)S(1)}, u32[]{:S(2)}) copy-start(f32[128]{0:T(128)S(1)} %add_rsqrt_fusion.1) | copy-start | bytes 1540
  13.3 198.1 %all-reduce.8.cloned.1.call-start = ((), (), s32[]{:S(2)}) async-start(), calls=%async_computation.2 | async-start | bytes 786432 | tf_op jit(solution)/shard_map/psum | solution.py:185
  15.0 112.1 %copy-start.17 = (s32[128]{0:T(128)S(1)}, s32[128]{0:T(128)}, u32[]{:S(2)}) copy-start(s32[128]{0:T(128)} %param.24) | copy-start | bytes 1540
  127.2 54.7 %copy-start.27 = (s32[128]{0:T(128)S(1)}, s32[128]{0:T(128)}, u32[]{:S(2)}) copy-start(s32[128]{0:T(128)} %param.25) | copy-start | bytes 1540
  127.2 84.2 %copy-start.4 = (bf16[128,768]{1,0:T(8,128)(2,1)S(1)}, bf16[128,768]{1,0:T(8,128)(2,1)}, u32[]{:S(2)}) copy-start(bf16[128,768]{1,0:T(8,128)(2,1)} %param.23) | copy-start | bytes 589828
  127.2 84.2 %copy-start.25 = (f32[768]{0:T(1024)S(1)}, f32[768]{0:T(1024)}, u32[]{:S(2)}) copy-start(f32[768]{0:T(1024)} %param.35) | copy-start | bytes 9220
  127.2 85.7 %copy-start.16 = (f32[768]{0:T(1024)S(1)}, f32[768]{0:T(1024)}, u32[]{:S(2)}) copy-start(f32[768]{0:T(1024)} %param.36) | copy-start | bytes 9220
  127.2 85.7 %copy-start.21 = (f32[768]{0:T(1024)S(1)}, f32[768]{0:T(1024)}, u32[]{:S(2)}) copy-start(f32[768]{0:T(1024)} %param.37) | copy-start | bytes 9220
  127.2 85.7 %copy-start.24 = (f32[1536]{0:T(1024)S(1)}, f32[1536]{0:T(1024)}, u32[]{:S(2)}) copy-start(f32[1536]{0:T(1024)} %param.39) | copy-start | bytes 18436
  179.4 2.4 copy-start.14
  179.4 36.6 %copy-start.9 = (bf16[128,768]{1,0:T(8,128)(2,1)S(1)}, bf16[128,768]{1,0:T(8,128)(2,1)}, u32[]{:S(2)}) copy-start(bf16[128,768]{1,0:T(8,128)(2,1)} %param.26) | copy-start | bytes 589828
  179.5 2.4 copy-start.12
  181.8 71.3 %all-reduce.10.cloned.1.call-start = ((), (), s32[]{:S(2)}) async-start(), calls=%async_computation.3 | async-start | bytes 786432 | tf_op jit(solution)/shard_map/psum | solution.py:208
  211.4 6.5 copy-start.5
  219.5 397.0 %reduce-scatter.2.cloned.1.call-start = ((), (), s32[]{:S(2)}) async-start(), calls=%async_computation.4 | async-start | bytes 25559040 | tf_op jit(solution)/shard_map/reduce_scatter | solution.py:258
  272.4 1.2 copy-start.2
  274.7 4.7 copy-start.1
  279.4 8.1 slice-start
  283.3 4.3 slice-start.1
  287.6 1.9 copy-start.3
  300.1 1.2 copy-start.2
  302.5 4.7 copy-start.1
  307.1 8.1 slice-start
  311.0 4.3 slice-start.1
  315.3 1.9 copy-start.3
  327.8 1.2 copy-start.2
  330.2 4.7 copy-start.1
  334.9 8.1 slice-start
  338.7 4.3 slice-start.1
  343.0 1.9 copy-start.3
  355.5 1.2 copy-start.2
  357.9 4.7 copy-start.1
  362.5 8.1 slice-start
  366.4 4.3 slice-start.1
  370.7 1.9 copy-start.3
  381.1 2.7 copy-start.6
  381.1 5.0 copy-start.15
  381.1 5.0 copy-start.18
  381.1 5.0 copy-start.20
  381.1 5.0 copy-start.23
  381.1 243.1 %copy-start.13 = (bf16[128,6,64]{0,2,1:T(8,128)(2,1)S(1)}, bf16[128,6,64]{0,2,1:T(8,128)(2,1)}, u32[]{:S(2)}) copy-start(bf16[128,6,64]{0,2,1:T(8,128)(2,1)} %copy-done.12) | copy-start | bytes 294916
  381.1 277.1 %all-reduce.14.cloned.1.call-start = ((), (), s32[]{:S(2)}) async-start(), calls=%async_computation.6 | async-start | bytes 786432 | tf_op jit(solution)/shard_map/psum | solution.py:194
  617.5 13.3 copy-start.10
  626.7 719.7 %all-reduce.12.cloned.1.call-start = ((), (), s32[]{:S(2)}) async-start(), calls=%async_computation.5 | async-start | bytes 28311552
  635.0 348.7 %copy-start.26 = (f32[768]{0:T(1024)S(1)}, f32[768]{0:T(1024)}, u32[]{:S(2)}) copy-start(f32[768]{0:T(1024)} %param.41) | copy-start | bytes 9220
  (4 other events, 3.1 us)
Sparse Core Ops, SparseCore 0:
  13.5 97.6 all-gather.1
  181.9 29.4 all-reduce.7
  219.6 33.4 all-reduce.9
  381.3 235.2 reduce-scatter.1
  626.9 31.3 all-reduce.13
  660.6 685.7 all-reduce.11
where the time goes:
time: 1360 us
  waiting for transfers between devices  770 us (57%)
  blocking collectives  324 us (24%)
  matrix products  138 us (10%)
  local copies, waits for them, and re-layouts  63.9 us (5%)
  other arithmetic  44.7 us (3%)
  between operations  15.2 us (1%)
    unnamed x7, waiting for transfers between devices  361 us
    psum x1, blocking collectives, on_device(): lax.psum((small_terms[0], small_terms[1], small_terms[2], small_terms[3],...  324 us
    reduce_scatter x1, waiting for transfers between devices, on_device(): lax.psum_scatter(pair_all, 'ctx', scatter_dimension=0, tiled=True)  229 us
    all_gather x1, waiting for transfers between devices, on_device(): shard_rows = lax.all_gather(key_value, 'ctx', axis=0, tiled=True)  96.1 us
    psum x1, waiting for transfers between devices, on_device(): lax.psum(lax.dot_general(dpre_low, up_weight, trans_right, preferred_elem...  33.3 us
    psum x1, waiting for transfers between devices, on_device(): lax.psum(jnp.dot(attn_low, o_weight, preferred_element_type=jnp.float32),...  29.6 us
    dynamic_update_slice x4, other arithmetic, accumulate(): lax.dynamic_update_slice_in_dim(pair_all, previous + addend, target, 0)  29 us
  transfers between devices with their start and end apart: 6, of which 6 were waited for; matrix products, arithmetic and copies ran while one was open for 1% of the time, Pallas kernels for 0%

commit v1 on v0

--- a/solution.py
+++ b/solution.py
@@ -3,10 +3,13 @@
 import jax
 import jax.numpy as jnp
 from jax import lax
-from jax.sharding import PartitionSpec as P
+from jax.sharding import Mesh, PartitionSpec as P
 
 HEAD_DIM = 64
 LAYER = 6
+CTX = ("x", "y", "zh", "core")
+CHIPS = ("x", "y", "zh")
+PLANE = ("x", "y")
 
 
 epsilon = 1e-05
@@ -53,6 +56,50 @@
         - jnp.mean(scaled, axis=-1, keepdims=True)
         - normed * jnp.mean(scaled * normed, axis=-1, keepdims=True)
     )
+
+
+def swap_add(part, axis):
+    other = lax.ppermute(part, axis, ((0, 1), (1, 0)))
+    return part.astype(jnp.float32) + other.astype(jnp.float32)
+
+
+def sum_vectors(vectors):
+    sizes = [vector.shape[0] for vector in vectors]
+    rows = jnp.concatenate(vectors).reshape(-1, 128)
+    rows = swap_add(rows, "core")
+    plane = lax.axis_size(PLANE)
+    copies = jnp.broadcast_to(rows[None], (plane,) + rows.shape)
+    rows = jnp.sum(lax.all_to_all(copies, PLANE, 0, 0, tiled=True), axis=0)
+    rows = swap_add(rows, "zh").reshape(-1)
+    ends = [sum(sizes[: i + 1]) for i in range(len(sizes))]
+    return [rows[end - size : end] for end, size in zip(ends, sizes, strict=True)]
+
+
+def sum_products(pairs):
+    parts = []
+    for left, right in pairs:
+        half = right.shape[1] // 2
+        left_chip = lax.all_gather(left, "core", axis=0, tiled=True)
+        right_chip = lax.all_to_all(right, "core", 1, 0, tiled=True)
+        parts.append(
+            lax.dot_general(
+                left_chip, right_chip, trans_left, preferred_element_type=jnp.float32
+            ).astype(jnp.bfloat16)
+        )
+    chips = lax.axis_size(CHIPS)
+    joined = jnp.concatenate(parts, axis=1)
+    joined = joined.reshape(chips, joined.shape[0] // chips, joined.shape[1])
+    received = lax.all_to_all(joined, CHIPS, 0, 0, tiled=True)
+    summed = jnp.sum(received.astype(jnp.float32), axis=0)
+    outs = []
+    begin = 0
+    for left, right in pairs:
+        half = right.shape[1] // 2
+        outs.append(
+            lax.all_to_all(summed[:, begin : begin + half], "core", 0, 1, tiled=True)
+        )
+        begin += half
+    return outs
 
 
 def by_blocks(step_fn, running, row_total):
@@ -116,13 +163,13 @@
     down_bias,
 ):
     per_device, model_width = tokens.shape
-    cycle_size = lax.axis_size("ctx")
+    cycle_size = lax.axis_size(CTX)
     stream_len = per_device * cycle_size
     local_width = q_weight.shape[1]
     local_heads = local_width // HEAD_DIM
     local_hidden = up_weight.shape[1]
     scaling = 1.0 / math.sqrt(HEAD_DIM)
-    cycle_index = lax.axis_index("ctx")
+    cycle_index = lax.axis_index(CTX)
     own_rows = cycle_index * per_device + jnp.arange(per_device, dtype=jnp.int32)
     query_place = stream_place(own_rows, per_device, stream_len)
     active = exit_layer > LAYER
@@ -158,7 +205,7 @@
         jnp.zeros((per_device, local_heads, HEAD_DIM), jnp.float32),
         jnp.zeros((per_device, local_heads), jnp.float32),
     )
-    shard_rows = lax.all_gather(key_value, "ctx", axis=0, tiled=True)
+    shard_rows = lax.all_gather(key_value, CTX, axis=0, tiled=True)
 
     def step_fn(state, offset, size_rows):
         block_kv = lax.dynamic_slice_in_dim(shard_rows, offset, size_rows, 0)
@@ -182,7 +229,7 @@
     attn_full = numerator / denominators[:, :, None]
     attn_low = attn_full.reshape(per_device, local_width).astype(jnp.bfloat16)
     attn_out = (
-        lax.psum(jnp.dot(attn_low, o_weight, preferred_element_type=jnp.float32), "wa") + o_bias
+        swap_add(jnp.dot(attn_low, o_weight, preferred_element_type=jnp.float32), "wa") + o_bias
     )
     middle = stream_in + attn_out
     normed_two, unit_two, inv_two = norm_forward(middle, ln2_gain, ln2_shift)
@@ -191,10 +238,10 @@
     hidden_full, gelu_slope = gelu_pair(pre_act)
     hidden = hidden_full.astype(jnp.bfloat16)
     ffn_out = (
-        lax.psum(
+        swap_add(
             jnp.dot(hidden, down_weight, preferred_element_type=jnp.float32).astype(jnp.bfloat16),
             "wa",
-        ).astype(jnp.float32)
+        )
         + down_bias
     )
     output = jnp.where(active[:, None], middle + ffn_out, stream_in).astype(jnp.bfloat16)
@@ -205,7 +252,7 @@
         branch_low, down_weight, trans_right, preferred_element_type=jnp.float32
     )
     dpre_low = (dhidden * gelu_slope).astype(jnp.bfloat16)
-    dnormed_two = lax.psum(
+    dnormed_two = swap_add(
         lax.dot_general(dpre_low, up_weight, trans_right, preferred_element_type=jnp.float32), "wa"
     )
     dmiddle = branch_grad + norm_backward(dnormed_two, unit_two, inv_two, ln2_gain)
@@ -219,7 +266,7 @@
         jnp.zeros((per_device, local_heads, HEAD_DIM), jnp.float32),
         jnp.zeros((stream_len, 2 * local_width), jnp.float32),
     )
-    key_shard_rows = lax.all_gather(key_value, "ctx", axis=0, tiled=True)
+    key_shard_rows = lax.all_gather(key_value, CTX, axis=0, tiled=True)
 
     def step_fn(state, offset, size_rows):
         block_kv = lax.dynamic_slice_in_dim(key_shard_rows, offset, size_rows, 0)
@@ -255,7 +302,7 @@
         return accumulate(state)
 
     query_acc, pair_all = by_blocks(step_fn, back_state, key_shard_rows.shape[0])
-    pair_sum = lax.psum_scatter(pair_all, "ctx", scatter_dimension=0, tiled=True)
+    pair_sum = lax.psum_scatter(pair_all, CTX, scatter_dimension=0, tiled=True)
     query_sum = query_acc.reshape(per_device, local_width)
     query_low = query_sum.astype(jnp.bfloat16)
     key_low = pair_sum[:, :local_width].astype(jnp.bfloat16)
@@ -265,7 +312,7 @@
         + lax.dot_general(key_low, k_weight, trans_right, preferred_element_type=jnp.float32)
         + lax.dot_general(value_low, v_weight, trans_right, preferred_element_type=jnp.float32)
     )
-    dnormed_one = lax.psum(dnormed_part.astype(jnp.bfloat16), "wa").astype(jnp.float32)
+    dnormed_one = swap_add(dnormed_part.astype(jnp.bfloat16), "wa")
     input_grad = (
         dmiddle
         + norm_backward(dnormed_one, unit_one, inv_one, ln1_gain)
@@ -292,52 +339,24 @@
         ln1_shift_grad,
         ln2_gain_grad,
         ln2_shift_grad,
-    ) = lax.psum(
+    ) = sum_vectors(small_terms)
+    (
+        q_weight_grad,
+        k_weight_grad,
+        v_weight_grad,
+        o_weight_grad_t,
+        up_weight_grad,
+        down_weight_grad_t,
+    ) = sum_products(
         (
-            small_terms[0],
-            small_terms[1],
-            small_terms[2],
-            small_terms[3],
-            small_terms[4],
-            small_terms[5],
-            small_terms[6],
-            small_terms[7],
-            small_terms[8],
-        ),
-        "ctx",
-    )
-    weight_sums = lax.psum_scatter(
-        jnp.concatenate(
-            [
-                lax.dot_general(
-                    lowered_one, query_low, trans_left, preferred_element_type=jnp.float32
-                ),
-                lax.dot_general(
-                    lowered_one, key_low, trans_left, preferred_element_type=jnp.float32
-                ),
-                lax.dot_general(
-                    lowered_one, value_low, trans_left, preferred_element_type=jnp.float32
-                ),
-                lax.dot_general(
-                    dattn_low, attn_low, trans_left, preferred_element_type=jnp.float32
-                ),
-                lax.dot_general(
-                    lowered_two, dpre_low, trans_left, preferred_element_type=jnp.float32
-                ),
-                lax.dot_general(branch_low, hidden, trans_left, preferred_element_type=jnp.float32),
-            ],
-            axis=1,
-        ),
-        "ctx",
-        scatter_dimension=0,
-        tiled=True,
-    )
-    q_weight_grad = weight_sums[:, :local_width]
-    k_weight_grad = weight_sums[:, local_width : 2 * local_width]
-    v_weight_grad = weight_sums[:, 2 * local_width : 3 * local_width]
-    o_weight_grad_t = weight_sums[:, 3 * local_width : 4 * local_width]
-    up_weight_grad = weight_sums[:, 4 * local_width : 4 * local_width + local_hidden]
-    down_weight_grad_t = weight_sums[:, 4 * local_width + local_hidden :]
+            (lowered_one, query_low),
+            (lowered_one, key_low),
+            (lowered_one, value_low),
+            (dattn_low, attn_low),
+            (lowered_two, dpre_low),
+            (branch_low, hidden),
+        )
+    )
     return (
         output,
         input_grad,
@@ -360,14 +379,15 @@
 
 
 def solution(mesh):
+    fine = Mesh(mesh.devices.reshape(4, 4, 2, 2, 2), CTX + ("wa",))
     return jax.shard_map(
         on_device,
-        mesh=mesh,
+        mesh=fine,
         in_specs=(
-            P("ctx", None),
-            P("ctx"),
-            P("ctx"),
-            P("ctx", None),
+            P(CTX, None),
+            P(CTX),
+            P(CTX),
+            P(CTX, None),
             P(),
             P(),
             P(None, "wa"),
@@ -385,22 +405,22 @@
             P(),
         ),
         out_specs=(
-            P("ctx", None),
-            P("ctx", None),
-            P(),
-            P(),
-            P("ctx", "wa"),
-            P("wa"),
-            P("ctx", "wa"),
-            P("ctx", "wa"),
-            P("wa"),
-            P("ctx", "wa"),
-            P(),
-            P(),
-            P(),
-            P("ctx", "wa"),
-            P("wa"),
-            P("ctx", "wa"),
+            P(CTX, None),
+            P(CTX, None),
+            P(),
+            P(),
+            P(CTX, "wa"),
+            P("wa"),
+            P(CTX, "wa"),
+            P(CTX, "wa"),
+            P("wa"),
+            P(CTX, "wa"),
+            P(),
+            P(),
+            P(),
+            P(CTX, "wa"),
+            P("wa"),
+            P(CTX, "wa"),
             P(),
         ),
         check_vma=False,

time: 1360 us -> 701 us (0.52)
  waiting for transfers between devices: 770 us -> 368 us
  blocking collectives: 324 us -> 42.1 us
  starting transfers between devices: 0.65 us -> 38.1 us
  matrix products: 138 us -> 120 us
    unnamed x7 -> x2, waiting for transfers between devices: 361 us -> 0.03 us
    psum x1 -> x0, blocking collectives: 324 us -> none  [on_device(): lax.psum((small_terms[0], small_terms[1], small_terms[2], small_terms[3],...]
    psum x3 -> x0, waiting for transfers between devices: 84.1 us -> none  [the longest x1 33.3 us: on_device(): lax.psum(lax.dot_general(dpre_low, up_weight, trans_right, preferred_elem...]
    ppermute x0 -> x6, waiting for transfers between devices: none -> 34 us  [swap_add(): other = lax.ppermute(part, axis, ((0, 1), (1, 0)))]
    all_to_all x0 -> x7, starting transfers between devices: none -> 32.5 us  [the longest x5 20.8 us: sum_products(): right_chip = lax.all_to_all(right, 'core', 1, 0, tiled=True)]
    all_to_all x0 -> x7, blocking collectives: none -> 29.8 us  [the longest x6 25.8 us: sum_products(): lax.all_to_all(summed[:, begin:begin + half], 'core', 0, 1, tiled=True)]
    all_to_all x0 -> x7, waiting for transfers between devices: none -> 26.3 us  [the longest x1 23.9 us: sum_products(): received = lax.all_to_all(joined, CHIPS, 0, 0, tiled=True)]
    reduce_scatter x1, waiting for transfers between devices: 229 us -> 211 us  [on_device(): pair_sum = lax.psum_scatter(pair_all, CTX, scatter_dimension=0, tiled=True)]
  transfers between devices with their start and end apart: 6 -> 15, of which waited for: 6 -> 11; matrix products, arithmetic and copies ran while one was open for 1% -> 4% of each run, Pallas kernels for 0% -> 0%
where the time goes in v1:
time: 701 us; the launch traced here: 699 us
  waiting for transfers between devices  368 us (52%)
  matrix products  120 us (17%)
  local copies, waits for them, and re-layouts  70.6 us (10%)
  other arithmetic  45.4 us (6%)
  blocking collectives  42.1 us (6%)
  starting transfers between devices  38.1 us (5%)
  between operations  14.7 us (2%)
    reduce_scatter x1, waiting for transfers between devices, on_device(): pair_sum = lax.psum_scatter(pair_all, CTX, scatter_dimension=0, tiled=True)  211 us
    all_gather x1, waiting for transfers between devices, on_device(): shard_rows = lax.all_gather(key_value, CTX, axis=0, tiled=True)  96.2 us
    ppermute x6, waiting for transfers between devices, swap_add(): other = lax.ppermute(part, axis, ((0, 1), (1, 0)))  34 us
    dynamic_update_slice x4, other arithmetic, accumulate(): lax.dynamic_update_slice_in_dim(pair_all, previous + addend, target, 0)  29 us
    all_to_all x6, blocking collectives, sum_products(): lax.all_to_all(summed[:, begin:begin + half], 'core', 0, 1, tiled=True)  25.8 us
    all_to_all x1, waiting for transfers between devices, sum_products(): received = lax.all_to_all(joined, CHIPS, 0, 0, tiled=True)  23.9 us
    dot_general x8, matrix products, attend_block(): jnp.einsum('qhd,khd->hqk', query_rows, key_rows, preferred_element_type=j...  22.7 us
    all_to_all x5, starting transfers between devices, sum_products(): right_chip = lax.all_to_all(right, 'core', 1, 0, tiled=True)  20.8 us
  transfers between devices with their start and end apart: 15, of which 11 were waited for; matrix products, arithmetic and copies ran while one was open for 4% of the time, Pallas kernels for 0%

profile of v1, /device:TPU:1, one launch (start us, length us, event | category | flops | bytes accessed | tf_op | source)
XLA Modules:
  0.0 699.0 jit_solution(11546718277282906590)
XLA Ops:
  16.3 96.2 %all-gather.2.cloned.1.call-done = bf16[8192,768]{1,0:T(8,128)(2,1)} async-done(((bf16[128,768]{1,0:T(8,128)(2,1)}), bf16[8192,768]{1,0:T(8,128)(2,1)}) %all-gather.2.cloned.1.call-update) | async-done | bytes 12582928 | tf_op jit(solution)/shard_map/all_gather | solution.py:208
  112.5 16.7 %copy.135 = bf16[8192,768]{0,1:T(8,128)(2,1)} copy(bf16[8192,768]{1,0:T(8,128)(2,1)} %all-gather.2.cloned.1.call-done) | data formatting | bytes 25165824
  129.2 52.2 %while.36 = (s32[]{:T(128)}, f32[128,6,64]{0,2,1:T(8,128)S(1)}, f32[128,6]{0,1:T(8,128)S(1)}, bf16[8192,768]{0,1:T(8,128)(2,1)}, s32[128]{0:T(128)S(1)}, /*index...) while((s32[]{:T(128)}, f32[128,6,64]{0,2,1:T(8,128)S(1)}, ...), condition=%wide.region_4.5_spmd.clone, body=%wide.region_2.4_spmd.clone.sunk | while | flops 413038976 | bytes 23328464 | solution.py:110
  129.2 3.5 constant_dynamic-slice_fusion.3
  133.1 4.5 fusion.177
  137.6 4.6 fusion.178
  146.1 4.5 fusion.177
  150.6 4.6 fusion.178
  159.1 4.5 fusion.177
  163.7 4.6 fusion.178
  172.2 4.5 fusion.177
  176.7 4.6 fusion.178
  184.1 10.0 %collective-permute-done = f32[128,768]{1,0:T(8,128)S(1)} collective-permute-done((f32[128,768]{1,0:T(8,128)S(1)}, f32[128,768]{1,0:T(8,128)S(1)}, u32[]{:S(2)}, u32[]{:S(2)}) %collective-permute-start) | collective-permute-done | bytes 393248 | tf_op jit(solution)/shard_map/ppermute | solution.py:62
  203.5 5.7 collective-permute-done.2
  215.0 11.4 %broadcast_in_dim.161 = f32[8192,768]{0,1:T(8,128)} broadcast(f32[]{:T(128)} %constant.316.clone.1), dimensions={} | broadcast | bytes 25165828 | tf_op jit(solution)/shard_map/broadcast_in_dim | solution.py:267
  226.5 101.8 %while.37 = (s32[]{:T(128)}, f32[128,6,64]{0,2,1:T(8,128)S(1)}, f32[8192,768]{0,1:T(8,128)}, bf16[8192,768]{0,1:T(8,128)(2,1)}, s32[128]{0:T(128)S(1)}, /*index=...) while((s32[]{:T(128)}, f32[128,6,64]{0,2,1:T(8,128)S(1)}, ...), condition=%wide.region_11.12_spmd.clone, body=%wide.region_10.11_spmd.clone.sunk | while | flops 1232992640 | bytes 135666512 | solution.py:110
  230.2 4.3 fusion.192
  237.3 4.3 fusion.194
  244.7 7.2 %fusion.195 = f32[8192,768]{0,1:T(8,128)} fusion(f32[8192,768]{0,1:T(8,128)} %get-tuple-element.869, s32[]{:T(128)S(6)} %select_n.332, f32[2048,384]{0,1:T(8,128)S(1)} %bitcast.235, f32[2048,384]{0,1:T(8,128)S(1)} %bitcast.234), kind=kLoop, calls=%fused_computation.36.clone.1 | loop fusion | flops 3145728 | bytes 18874372 | tf_op jit(solution)/shard_map/while/body/eval_jaxpr/dynamic_update_slice | solution.py:299
  255.7 4.3 fusion.192
  262.7 4.3 fusion.194
  270.1 7.2 %fusion.195 = f32[8192,768]{0,1:T(8,128)} fusion(f32[8192,768]{0,1:T(8,128)} %get-tuple-element.869, s32[]{:T(128)S(6)} %select_n.332, f32[2048,384]{0,1:T(8,128)S(1)} %bitcast.235, f32[2048,384]{0,1:T(8,128)S(1)} %bitcast.234), kind=kLoop, calls=%fused_computation.36.clone.1 | loop fusion | flops 3145728 | bytes 18874372 | tf_op jit(solution)/shard_map/while/body/eval_jaxpr/dynamic_update_slice | solution.py:299
  281.1 4.3 fusion.192
  288.2 4.3 fusion.194
  295.6 7.3 %fusion.195 = f32[8192,768]{0,1:T(8,128)} fusion(f32[8192,768]{0,1:T(8,128)} %get-tuple-element.869, s32[]{:T(128)S(6)} %select_n.332, f32[2048,384]{0,1:T(8,128)S(1)} %bitcast.235, f32[2048,384]{0,1:T(8,128)S(1)} %bitcast.234), kind=kLoop, calls=%fused_computation.36.clone.1 | loop fusion | flops 3145728 | bytes 18874372 | tf_op jit(solution)/shard_map/while/body/eval_jaxpr/dynamic_update_slice | solution.py:299
  306.6 4.3 fusion.192
  313.7 4.3 fusion.194
  321.0 7.2 %fusion.195 = f32[8192,768]{0,1:T(8,128)} fusion(f32[8192,768]{0,1:T(8,128)} %get-tuple-element.869, s32[]{:T(128)S(6)} %select_n.332, f32[2048,384]{0,1:T(8,128)S(1)} %bitcast.235, f32[2048,384]{0,1:T(8,128)S(1)} %bitcast.234), kind=kLoop, calls=%fused_computation.36.clone.1 | loop fusion | flops 3145728 | bytes 18874372 | tf_op jit(solution)/shard_map/while/body/eval_jaxpr/dynamic_update_slice | solution.py:299
  329.2 3.7 all_gather.19
  337.2 4.0 all_gather.21
  342.0 3.5 all-to-all-start.1
  350.6 211.1 %reduce-scatter.2.cloned.1.call-done = f32[128,768]{0,1:T(8,128)} async-done(((f32[8192,768]{0,1:T(8,128)}), f32[128,768]{0,1:T(8,128)}) %reduce-scatter.2.cloned.1.call-update) | async-done | bytes 393232 | tf_op jit(solution)/shard_map/reduce_scatter | solution.py:305
  565.8 6.1 all-to-all-start.2
  573.0 3.7 all-to-all-start.3
  577.7 3.7 all-to-all-start.4
  582.9 3.9 all-to-all-start.5
  588.1 4.0 all_to_all.232
  592.9 4.1 all-to-all-start
  600.1 5.8 copy.145
  606.8 7.6 %all-to-all-start.7 = ((bf16[32,24,2304]{2,1,0:T(8,128)(2,1)}), bf16[32,24,2304]{2,1,0:T(8,128)(2,1)}, u32[]{:S(2)}, u32[]{:S(2)}) async-start(bf16[32,24,2304]{2,1,0:T(8,128)(2,1)} %bitcast.241), calls=%async_computation.8 | async-start | bytes 7077888 | tf_op jit(solution)/shard_map/all_to_all | solution.py:92
  618.2 15.4 %collective-permute-done.5 = f32[54,128]{1,0:T(8,128)S(1)} collective-permute-done((f32[54,128]{1,0:T(8,128)S(1)}, f32[54,128]{1,0:T(8,128)S(1)}, u32[]{:S(2)}, u32[]{:S(2)}) %collective-permute-start.5) | collective-permute-done | bytes 27680 | tf_op jit(solution)/shard_map/ppermute | solution.py:62
  635.4 23.9 %all-to-all-done.7 = bf16[32,24,2304]{2,1,0:T(8,128)(2,1)} async-done(((bf16[32,24,2304]{2,1,0:T(8,128)(2,1)}), bf16[32,24,2304]{2,1,0:T(8,128)(2,1)}, u32[]{:S(2)}, u32[]{:S(2)}) %all-to-all-start.7) | async-done | bytes 3538976 | tf_op jit(solution)/shard_map/all_to_all | solution.py:92
  662.0 7.0 %all_to_all.233 = f32[2,12,192]{2,1,0:T(8,128)S(1)} all-to-all(f32[2,12,192]{2,1,0:T(8,128)S(1)} %all_to_all.194), channel_id=1, replica_groups=mesh['x'=4,'y'=4,'zh'=2,'core'=2,'wa'=2] {'core'}, dimensions={0} | all-to-all | bytes 36864 | tf_op jit(solution)/shard_map/all_to_all | solution.py:99
  669.7 3.7 all_to_all.234
  674.2 3.7 all_to_all.235
  678.6 3.7 all_to_all.236
  683.1 3.8 all_to_all.237
  687.6 3.8 all_to_all.238
  (268 shorter events, 114.2 us)
Async XLA Ops:
  7.2 187.4 %copy-start = (bf16[768,1536]{1,0:T(8,128)(2,1)S(1)}, bf16[768,1536]{1,0:T(8,128)(2,1)}, u32[]{:S(2)}) copy-start(bf16[768,1536]{1,0:T(8,128)(2,1)} %param.38) | copy-start | bytes 7077892
  7.2 105.3 %all-gather.2.cloned.1.call-start = ((), (), s32[]{:S(2)}) async-start(), calls=%async_computation.15 | async-start | bytes 12779520 | tf_op jit(solution)/shard_map/all_gather | solution.py:208
  14.7 546.9 %reduce-scatter.2.cloned.1.call-start = ((), (), s32[]{:S(2)}) async-start(), calls=%async_computation.16 | async-start | bytes 25559040 | tf_op jit(solution)/shard_map/reduce_scatter | solution.py:305
  16.3 112.9 %copy-start.22 = (s32[128]{0:T(128)S(1)}, s32[128]{0:T(128)}, u32[]{:S(2)}) copy-start(s32[128]{0:T(128)} %param.24) | copy-start | bytes 1540
  129.1 54.8 %copy-start.33 = (s32[128]{0:T(128)S(1)}, s32[128]{0:T(128)}, u32[]{:S(2)}) copy-start(s32[128]{0:T(128)} %param.25) | copy-start | bytes 1540
  129.1 54.8 %copy-start.11 = (bf16[128,768]{1,0:T(8,128)(2,1)S(1)}, bf16[128,768]{1,0:T(8,128)(2,1)}, u32[]{:S(2)}) copy-start(bf16[128,768]{1,0:T(8,128)(2,1)} %param.26) | copy-start | bytes 589828
  129.2 64.9 %copy-start.4 = (bf16[128,768]{1,0:T(8,128)(2,1)S(1)}, bf16[128,768]{1,0:T(8,128)(2,1)}, u32[]{:S(2)}) copy-start(bf16[128,768]{1,0:T(8,128)(2,1)} %param.23) | copy-start | bytes 589828
  129.2 64.9 %copy-start.29 = (f32[768]{0:T(1024)S(1)}, f32[768]{0:T(1024)}, u32[]{:S(2)}) copy-start(f32[768]{0:T(1024)} %param.35) | copy-start | bytes 9220
  181.4 14.6 %copy-start.17 = (f32[128,6,64]{0,2,1:T(8,128)}, f32[128,6,64]{0,2,1:T(8,128)S(1)}, u32[]{:S(2)}) copy-start(f32[128,6,64]{0,2,1:T(8,128)S(1)} %get-tuple-element.445) | copy-start | bytes 589828
  181.4 13.1 %copy-start.23 = (f32[768]{0:T(1024)S(1)}, f32[768]{0:T(1024)}, u32[]{:S(2)}) copy-start(f32[768]{0:T(1024)} %param.36) | copy-start | bytes 9220
  181.4 13.0 %copy-start.30 = (f32[768]{0:T(1024)S(1)}, f32[768]{0:T(1024)}, u32[]{:S(2)}) copy-start(f32[768]{0:T(1024)} %param.37) | copy-start | bytes 9220
  181.4 13.2 %copy-start.32 = (f32[1536]{0:T(1024)S(1)}, f32[1536]{0:T(1024)}, u32[]{:S(2)}) copy-start(f32[1536]{0:T(1024)} %param.39) | copy-start | bytes 18436
  183.5 12.5 %copy-start.8 = (bf16[1536,768]{1,0:T(8,128)(2,1)S(1)}, bf16[1536,768]{1,0:T(8,128)(2,1)}, u32[]{:S(2)}) copy-start(bf16[1536,768]{1,0:T(8,128)(2,1)} %param.40) | copy-start | bytes 7077892
  183.5 10.5 %collective-permute-start = (f32[128,768]{1,0:T(8,128)S(1)}, f32[128,768]{1,0:T(8,128)S(1)}, u32[]{:S(2)}, u32[]{:S(2)}) collective-permute-start(f32[128,768]{1,0:T(8,128)S(1)} %fusion.102), channel_id=1, source_target_pairs={{0,1},{1,0},{2,3},{3,2},{4,5},{5,4},{6,7},{7,6},{8,9},{9,8},{10,11... | collective-permute-start | bytes 1179656 | tf_op jit(solution)/shard_map/ppermute | solution.py:62
  184.1 12.9 %copy-start.19 = (bf16[128,768]{1,0:T(8,128)(2,1)}, bf16[128,768]{1,0:T(8,128)(2,1)S(1)}, u32[]{:S(2)}) copy-start(bf16[128,768]{1,0:T(8,128)(2,1)S(1)} %fusion.64) | copy-start | bytes 589828
  197.8 15.6 %copy-start.31 = (f32[768]{0:T(1024)S(1)}, f32[768]{0:T(1024)}, u32[]{:S(2)}) copy-start(f32[768]{0:T(1024)} %param.41) | copy-start | bytes 9220
  199.4 15.1 %copy-start.9 = (bf16[384,768]{1,0:T(8,128)(2,1)S(1)}, bf16[384,768]{1,0:T(8,128)(2,1)}, u32[]{:S(2)}) copy-start(bf16[384,768]{1,0:T(8,128)(2,1)} %param.34) | copy-start | bytes 1769476
  199.4 9.7 %collective-permute-start.2 = (f32[128,768]{1,0:T(8,128)}, f32[128,768]{1,0:T(8,128)S(1)}, u32[]{:S(2)}, u32[]{:S(2)}) collective-permute-start(f32[128,768]{1,0:T(8,128)} %fusion.103), channel_id=1, source_target_pairs={{0,1},{1,0},{2,3},{3,2},{4,5},{5,4},{6,7},{7,6},{8,9},{9,8},{10,11... | collective-permute-start | bytes 1179656 | tf_op jit(solution)/shard_map/ppermute | solution.py:62
  199.8 15.1 %copy-start.18 = (f32[128,6,64]{0,2,1:T(8,128)S(1)}, f32[128,6,64]{0,2,1:T(8,128)}, u32[]{:S(2)}) copy-start(f32[128,6,64]{0,2,1:T(8,128)} %copy-done.17) | copy-start | bytes 589828
  202.1 11.3 %collective-permute-start.1 = (bf16[128,768]{1,0:T(8,128)(2,1)S(1)}, bf16[128,768]{1,0:T(8,128)(2,1)S(1)}, u32[]{:S(2)}, u32[]{:S(2)}) collective-permute-start(bf16[128,768]{1,0:T(8,128)(2,1)S(1)} %convolution_convert_fusion.6), channel_id=1, source_target_pairs={{0,1},{1,0},{2,3},{3,2},{4,5},{5,4},{6,7},{7,6},{8,9},{9,8},{10,11... | collective-permute-start | bytes 589832 | tf_op jit(solution)/shard_map/ppermute | solution.py:62
  229.8 4.7 copy-start.2
  234.5 7.0 %slice-start = ((s8[6291456]{0:T(1024)(128)(4,1)}), s8[4194304]{0:T(1024)(128)(4,1)S(1)}, s32[]{:S(2)}) async-start(s8[6291456]{0:T(1024)(128)(4,1)} %bitcast.230), calls=%async_computation.17 | async-start | bytes 8388608 | tf_op jit(solution)/shard_map/while
  255.2 4.7 copy-start.2
  260.0 7.0 %slice-start = ((s8[6291456]{0:T(1024)(128)(4,1)}), s8[4194304]{0:T(1024)(128)(4,1)S(1)}, s32[]{:S(2)}) async-start(s8[6291456]{0:T(1024)(128)(4,1)} %bitcast.230), calls=%async_computation.17 | async-start | bytes 8388608 | tf_op jit(solution)/shard_map/while
  280.7 4.7 copy-start.2
  285.4 7.0 %slice-start = ((s8[6291456]{0:T(1024)(128)(4,1)}), s8[4194304]{0:T(1024)(128)(4,1)S(1)}, s32[]{:S(2)}) async-start(s8[6291456]{0:T(1024)(128)(4,1)} %bitcast.230), calls=%async_computation.17 | async-start | bytes 8388608 | tf_op jit(solution)/shard_map/while
  306.2 4.7 copy-start.2
  310.9 7.0 %slice-start = ((s8[6291456]{0:T(1024)(128)(4,1)}), s8[4194304]{0:T(1024)(128)(4,1)S(1)}, s32[]{:S(2)}) async-start(s8[6291456]{0:T(1024)(128)(4,1)} %bitcast.230), calls=%async_computation.17 | async-start | bytes 8388608 | tf_op jit(solution)/shard_map/while
  328.3 7.1 %copy-start.13 = (bf16[128,1536]{1,0:T(8,128)(2,1)S(1)}, bf16[128,1536]{1,0:T(8,128)(2,1)}, u32[]{:S(2)}) copy-start(bf16[128,1536]{1,0:T(8,128)(2,1)} %copy-done.12) | copy-start | bytes 1179652
  328.3 20.2 %copy-start.10 = (bf16[768,384]{1,0:T(8,128)(2,1)S(1)}, bf16[768,384]{1,0:T(8,128)(2,1)}, u32[]{:S(2)}) copy-start(bf16[768,384]{1,0:T(8,128)(2,1)} %param.29) | copy-start | bytes 1769476
  336.1 228.8 %copy-start.7 = (bf16[768,384]{1,0:T(8,128)(2,1)S(1)}, bf16[768,384]{1,0:T(8,128)(2,1)}, u32[]{:S(2)}) copy-start(bf16[768,384]{1,0:T(8,128)(2,1)} %param.32) | copy-start | bytes 1769476
  342.0 5.5 all-to-all-start.1
  348.5 233.9 %copy-start.24 = (f32[768]{0:T(1024)S(1)}, f32[768]{0:T(1024)}, u32[]{:S(2)}) copy-start(f32[768]{0:T(1024)} %param.27) | copy-start | bytes 9220
  348.5 233.9 %copy-start.26 = (f32[128]{0:T(128)S(1)}, f32[128]{0:T(128)}, u32[]{:S(2)}) copy-start(f32[128]{0:T(128)} %copy-done.25) | copy-start | bytes 1540
  348.5 233.9 %copy-start.28 = (f32[128]{0:T(128)S(1)}, f32[128]{0:T(128)}, u32[]{:S(2)}) copy-start(f32[128]{0:T(128)} %copy-done.27) | copy-start | bytes 1540
  565.3 31.7 %copy-start.15 = (bf16[256,768]{1,0:T(8,128)(2,1)S(1)}, bf16[256,768]{1,0:T(8,128)(2,1)}, u32[]{:S(2)}) copy-start(bf16[256,768]{1,0:T(8,128)(2,1)} %all_gather.21) | copy-start | bytes 1179652
  565.3 17.1 %collective-permute-start.3 = (bf16[128,768]{1,0:T(8,128)(2,1)S(1)}, bf16[128,768]{1,0:T(8,128)(2,1)S(1)}, u32[]{:S(2)}, u32[]{:S(2)}) collective-permute-start(bf16[128,768]{1,0:T(8,128)(2,1)S(1)} %fusion.54), channel_id=1, source_target_pairs={{0,1},{1,0},{2,3},{3,2},{4,5},{5,4},{6,7},{7,6},{8,9},{9,8},{10,11... | collective-permute-start | bytes 589832 | tf_op jit(solution)/shard_map/ppermute | solution.py:62
  565.8 7.2 %all-to-all-start.2 = ((bf16[128,2,192]{0,2,1:T(8,128)(2,1)}), bf16[128,2,192]{0,2,1:T(8,128)(2,1)S(1)}, u32[]{:S(2)}, u32[]{:S(2)}) async-start(bf16[128,2,192]{0,2,1:T(8,128)(2,1)} %bitcast.9), calls=%async_computation.3 | async-start | bytes 196608 | tf_op jit(solution)/shard_map/all_to_all | solution.py:83
  573.0 4.8 all-to-all-start.3
  577.7 5.1 all-to-all-start.4
  581.4 17.2 %copy-start.14 = (bf16[256,768]{1,0:T(8,128)(2,1)S(1)}, bf16[256,768]{1,0:T(8,128)(2,1)}, u32[]{:S(2)}) copy-start(bf16[256,768]{1,0:T(8,128)(2,1)} %all_gather.22) | copy-start | bytes 1179652
  582.7 5.0 collective-permute-start.4
  582.9 5.2 all-to-all-start.5
  592.9 13.9 %all-to-all-start = ((f32[16,54,128]{2,1,0:T(8,128)}), f32[16,54,128]{2,1,0:T(8,128)S(1)}, u32[]{:S(2)}, u32[]{:S(2)}) async-start(f32[16,54,128]{2,1,0:T(8,128)} %broadcast_in_dim.162), calls=%async_computation.1 | async-start | bytes 917504 | tf_op jit(solution)/shard_map/all_to_all | solution.py:72
  606.8 10.4 %copy-start.16 = (f32[128,768]{1,0:T(8,128)S(1)}, f32[128,768]{1,0:T(8,128)}, u32[]{:S(2)}) copy-start(f32[128,768]{1,0:T(8,128)} %get-tuple-element.658) | copy-start | bytes 1179652
  606.8 52.5 %all-to-all-start.7 = ((bf16[32,24,2304]{2,1,0:T(8,128)(2,1)}), bf16[32,24,2304]{2,1,0:T(8,128)(2,1)}, u32[]{:S(2)}, u32[]{:S(2)}) async-start(bf16[32,24,2304]{2,1,0:T(8,128)(2,1)} %bitcast.241), calls=%async_computation.8 | async-start | bytes 7077888 | tf_op jit(solution)/shard_map/all_to_all | solution.py:92
  614.5 19.1 %collective-permute-start.5 = (f32[54,128]{1,0:T(8,128)S(1)}, f32[54,128]{1,0:T(8,128)S(1)}, u32[]{:S(2)}, u32[]{:S(2)}) collective-permute-start(f32[54,128]{1,0:T(8,128)S(1)} %reduce_sum.217), channel_id=1, source_target_pairs={{0,4},{4,0},{1,5},{5,1},{2,6},{6,2},{3,7},{7,3},{8,12},{12,8},{9,1... | collective-permute-start | bytes 82952 | tf_op jit(solution)/shard_map/ppermute | solution.py:62
  634.2 58.0 %copy-start.1 = (bf16[768,1536]{1,0:T(8,128)(2,1)S(1)}, bf16[768,1536]{1,0:T(8,128)(2,1)}, u32[]{:S(2)}) copy-start(bf16[768,1536]{1,0:T(8,128)(2,1)} %param.38) | copy-start | bytes 7077892
  (15 other events, 37.6 us)
Sparse Core Ops, SparseCore 0:
  14.8 97.5 all-gather.1
  328.4 233.1 reduce-scatter.1
